TPU v7x, 32 devices: a whole 2x2x4 slice. The times are simulated.
32 devices in a mesh: dp: 8 (over z, x), tensor: 4 (over y, core).
Axes of the slice: x: 2, y: 2, z: 4, core: 2. Of those that a mesh axis runs over, the one named last changes fastest.
Arguments:
- tokens: bfloat16 [4672, 768], P('dp'), may hold values from -6 to 6
- segment_ids: int32 [8, 584], P('dp'), may hold values from 0 to 2, never falling along the last dimension, each value on 1 to 511 neighbouring positions
- norm1_gain: float32 [2, 768], replicated, may hold values from 0.5 to 1.5
- norm1_shift: float32 [2, 768], replicated, may hold values from -1.75 to 1.75
- qkv_weight: bfloat16 [2, 768, 2304], P(None, None, 'tensor'), may hold values from -0.21875 to 0.21875
- qv_bias: float32 [2, 12, 128], P(None, 'tensor'), may hold values from -3 to 3
- out_weight: bfloat16 [2, 768, 768], P(None, 'tensor'), may hold values from -0.625 to 0.625
- out_bias: float32 [2, 768], replicated, may hold values from -1.75 to 1.75
- norm2_gain: float32 [2, 768], replicated, may hold values from 0.2 to 1.8
- norm2_shift: float32 [2, 768], replicated, may hold values from -1.75 to 1.75
- fc1_weight: bfloat16 [2, 768, 3072], P(None, None, 'tensor'), may hold values from -0.21875 to 0.21875
- fc1_bias: float32 [2, 3072], P(None, 'tensor'), may hold values from -3 to 3
- fc2_weight: bfloat16 [2, 3072, 768], P(None, 'tensor'), may hold values from -0.21875 to 0.21875
- fc2_bias: float32 [2, 768], replicated, may hold values from -3.5 to 3.5
- cotangent: bfloat16 [4672, 768], P('dp'), may hold values from -6 to 6
Outputs:
- output: float32 [4672, 768], P('dp')
- input_grad: float32 [4672, 768], P('dp')
- norm1_gain_grad: float32 [2, 768], P(None, 'dp')
- norm1_shift_grad: float32 [2, 768], P(None, 'dp')
- qkv_weight_grad: float32 [2, 768, 2304], P(None, 'dp', 'tensor')
- qv_bias_grad: float32 [2, 12, 128], P(None, 'tensor', 'dp')
- out_weight_grad: float32 [2, 768, 768], P(None, 'tensor', 'dp')
- out_bias_grad: float32 [2, 768], P(None, 'dp')
- norm2_gain_grad: float32 [2, 768], P(None, 'dp')
- norm2_shift_grad: float32 [2, 768], P(None, 'dp')
- fc1_weight_grad: float32 [2, 768, 3072], P(None, 'dp', 'tensor')
- fc1_bias_grad: float32 [2, 3072], P(None, ('tensor', 'dp'))
- fc2_weight_grad: float32 [2, 3072, 768], P(None, 'tensor', 'dp')
- fc2_bias_grad: float32 [2, 768], P(None, 'dp')
Inputs may be any that keep to these rules, and one draw needn't show every extreme that they name: `segment_ids`: along each packed row the ids never fall; the tokens of a row with equal ids belong to one document.
All inputs are finite; a program needn't handle non-finite values.
Results may differ from a plain program's by a relative error of at most 0.028.
Values may be sent and summed in bfloat16 or wider, within the bound.
A program may use at most 128 MiB of HBM per device.

v0:
```python
import jax
import jax.numpy as jnp
from jax import lax
from jax.sharding import PartitionSpec as P

NORM_EPS = 1e-05
GELU_C = 0.7978845608028654
NEG_FILL = -1e30


def layer_norm(hidden, norm_gain, norm_shift):
    row_mean = jnp.mean(hidden, axis=-1, keepdims=True)
    centred = hidden - row_mean
    variance = jnp.mean(centred * centred, axis=-1, keepdims=True)
    inverse = lax.rsqrt(variance + NORM_EPS)
    normal = centred * inverse
    return (normal * norm_gain + norm_shift, normal, inverse)


def norm_backward(grad_out, normal, inverse, norm_gain):
    scaled = grad_out * norm_gain
    return inverse * (
        scaled
        - jnp.mean(scaled, axis=-1, keepdims=True)
        - normal * jnp.mean(scaled * normal, axis=-1, keepdims=True)
    )


def gelu_pair(preact):
    inner_arg = GELU_C * (preact + 0.044715 * preact * preact * preact)
    tanh_value = jnp.tanh(inner_arg)
    gelu_out = 0.5 * preact * (1.0 + tanh_value)
    gelu_slope = 0.5 * (1.0 + tanh_value) + 0.5 * preact * (
        1.0 - tanh_value * tanh_value
    ) * GELU_C * (1.0 + 3.0 * 0.044715 * preact * preact)
    return (gelu_out, gelu_slope)


def branch_total(partial_sum):
    return lax.psum(partial_sum.astype(jnp.bfloat16), "tensor").astype(jnp.float32)


def input_total(partial_sum):
    return lax.psum(partial_sum.astype(jnp.bfloat16), "tensor").astype(jnp.float32)


def sum_blocks(grads):
    return (
        lax.psum_scatter(grads[0], "dp", scatter_dimension=1, tiled=True),
        lax.psum_scatter(grads[1], "dp", scatter_dimension=1, tiled=True),
        lax.psum_scatter(grads[2], "dp", scatter_dimension=1, tiled=True),
        lax.psum_scatter(grads[3], "dp", scatter_dimension=2, tiled=True),
        lax.psum_scatter(grads[4], "dp", scatter_dimension=2, tiled=True),
        lax.psum_scatter(grads[5], "dp", scatter_dimension=1, tiled=True),
        lax.psum_scatter(grads[6], "dp", scatter_dimension=1, tiled=True),
        lax.psum_scatter(grads[7], "dp", scatter_dimension=1, tiled=True),
        lax.psum_scatter(grads[8], "dp", scatter_dimension=1, tiled=True),
        lax.psum_scatter(grads[9], "dp", scatter_dimension=1, tiled=True),
        lax.psum_scatter(grads[10], "dp", scatter_dimension=2, tiled=True),
        lax.psum_scatter(grads[11], "dp", scatter_dimension=1, tiled=True),
    )


def attend_scores(queries, key_vecs, allowed):
    score_scale = queries.shape[-1] ** (-0.5)
    scores = (
        jnp.einsum("rqhd,rkhd->rhqk", queries, key_vecs, preferred_element_type=jnp.float32)
        * score_scale
    )
    return jnp.where(allowed, scores, NEG_FILL)


def forward_layer(hidden, allowed, params, batch_rows):
    (
        gain_one,
        shift_one,
        qkv_w,
        qv_b,
        out_w,
        out_b,
        gain_two,
        shift_two,
        up_w,
        up_b,
        down_w,
        down_b,
    ) = params
    tok_count = hidden.shape[0]
    local_heads = qv_b.shape[0]
    head_size = qv_b.shape[1] // 2
    normed, normal_one, inverse_one = layer_norm(hidden, gain_one, shift_one)
    normed_b = normed.astype(jnp.bfloat16)
    projected = jnp.dot(normed_b, qkv_w, preferred_element_type=jnp.float32)
    projected = projected.reshape(batch_rows, tok_count // batch_rows, local_heads, 3, head_size)
    queries = (projected[:, :, :, 0] + qv_b[:, :head_size]).astype(jnp.bfloat16)
    key_vecs = projected[:, :, :, 1].astype(jnp.bfloat16)
    values = (projected[:, :, :, 2] + qv_b[:, head_size:]).astype(jnp.bfloat16)
    scores = attend_scores(queries, key_vecs, allowed)
    row_top = jnp.max(scores, axis=-1, keepdims=True)
    log_total = row_top + jnp.log(jnp.sum(jnp.exp(scores - row_top), axis=-1, keepdims=True))
    weights = jnp.exp(scores - log_total).astype(jnp.bfloat16)
    mixed_heads = jnp.einsum("rhqk,rkhd->rqhd", weights, values, preferred_element_type=jnp.float32)
    mixed_heads = mixed_heads.astype(jnp.bfloat16).reshape(tok_count, local_heads * head_size)
    after_attn = (
        hidden
        + branch_total(jnp.dot(mixed_heads, out_w, preferred_element_type=jnp.float32))
        + out_b
    )
    middle, normal_two, inverse_two = layer_norm(after_attn, gain_two, shift_two)
    mid_b = middle.astype(jnp.bfloat16)
    preact = jnp.dot(mid_b, up_w, preferred_element_type=jnp.float32) + up_b
    gelu_out, gelu_slope = gelu_pair(preact)
    gelu_b = gelu_out.astype(jnp.bfloat16)
    block_out = (
        after_attn
        + branch_total(jnp.dot(gelu_b, down_w, preferred_element_type=jnp.float32))
        + down_b
    )
    saved = (
        normed_b,
        normal_one,
        inverse_one,
        queries,
        key_vecs,
        values,
        log_total,
        mixed_heads,
        normal_two,
        inverse_two,
        mid_b,
        gelu_slope,
        gelu_b,
    )
    return (block_out, saved)


def backward_layer(grad_out, allowed, params, saved, batch_rows):
    (
        gain_one,
        shift_one,
        qkv_w,
        qv_b,
        out_w,
        out_b,
        gain_two,
        shift_two,
        up_w,
        up_b,
        down_w,
        down_b,
    ) = params
    (
        normed_b,
        normal_one,
        inverse_one,
        queries,
        key_vecs,
        values,
        log_total,
        mixed_heads,
        normal_two,
        inverse_two,
        mid_b,
        gelu_slope,
        gelu_b,
    ) = saved
    tok_count = grad_out.shape[0]
    local_heads = qv_b.shape[0]
    head_size = qv_b.shape[1] // 2
    score_scale = head_size ** (-0.5)
    down_b_grad = jnp.sum(grad_out, axis=0)
    grad_out_b = grad_out.astype(jnp.bfloat16)
    down_w_grad = jnp.einsum("nf,nd->fd", gelu_b, grad_out_b, preferred_element_type=jnp.float32)
    gelu_grad = jnp.einsum("nd,fd->nf", grad_out_b, down_w, preferred_element_type=jnp.float32)
    pre_grad = gelu_grad * gelu_slope
    up_b_grad = jnp.sum(pre_grad, axis=0)
    pre_grad_b = pre_grad.astype(jnp.bfloat16)
    up_w_grad = jnp.einsum("nd,nf->df", mid_b, pre_grad_b, preferred_element_type=jnp.float32)
    mid_grad = input_total(
        jnp.einsum("nf,df->nd", pre_grad_b, up_w, preferred_element_type=jnp.float32)
    )
    gain_two_grad = jnp.sum(mid_grad * normal_two, axis=0)
    shift_two_grad = jnp.sum(mid_grad, axis=0)
    resid_grad = grad_out + norm_backward(mid_grad, normal_two, inverse_two, gain_two)
    out_b_grad = jnp.sum(resid_grad, axis=0)
    resid_b = resid_grad.astype(jnp.bfloat16)
    out_w_grad = jnp.einsum("nk,nd->kd", mixed_heads, resid_b, preferred_element_type=jnp.float32)
    heads_grad = jnp.einsum("nd,kd->nk", resid_b, out_w, preferred_element_type=jnp.float32).astype(
        jnp.bfloat16
    )
    heads_grad = heads_grad.reshape(batch_rows, tok_count // batch_rows, local_heads, head_size)
    scores = attend_scores(queries, key_vecs, allowed)
    probs = jnp.exp(scores - log_total)
    probs_b = probs.astype(jnp.bfloat16)
    prob_grad = jnp.einsum(
        "rqhd,rkhd->rhqk", heads_grad, values, preferred_element_type=jnp.float32
    )
    mixed_four = mixed_heads.reshape(batch_rows, tok_count // batch_rows, local_heads, head_size)
    row_dots = jnp.sum(heads_grad.astype(jnp.float32) * mixed_four.astype(jnp.float32), axis=-1)
    row_dots = jnp.transpose(row_dots, (0, 2, 1))[..., None]
    score_grad = (probs * (prob_grad - row_dots) * score_scale).astype(jnp.bfloat16)
    query_grad = jnp.einsum(
        "rhqk,rkhd->rqhd", score_grad, key_vecs, preferred_element_type=jnp.float32
    )
    key_grad = jnp.einsum(
        "rhqk,rqhd->rkhd", score_grad, queries, preferred_element_type=jnp.float32
    )
    value_grad = jnp.einsum(
        "rhqk,rqhd->rkhd", probs_b, heads_grad, preferred_element_type=jnp.float32
    )
    qv_b_grad = jnp.concatenate(
        [jnp.sum(query_grad, axis=(0, 1)), jnp.sum(value_grad, axis=(0, 1))], axis=-1
    )
    proj_grad = jnp.stack([query_grad, key_grad, value_grad], axis=3).astype(jnp.bfloat16)
    proj_grad = proj_grad.reshape(tok_count, local_heads * 3 * head_size)
    qkv_w_grad = jnp.einsum("nd,nc->dc", normed_b, proj_grad, preferred_element_type=jnp.float32)
    normed_grad = input_total(
        jnp.einsum("nc,dc->nd", proj_grad, qkv_w, preferred_element_type=jnp.float32)
    )
    gain_one_grad = jnp.sum(normed_grad * normal_one, axis=0)
    shift_one_grad = jnp.sum(normed_grad, axis=0)
    input_grad = resid_grad + norm_backward(normed_grad, normal_one, inverse_one, gain_one)
    grads = (
        gain_one_grad,
        shift_one_grad,
        qkv_w_grad,
        qv_b_grad,
        out_w_grad,
        out_b_grad,
        gain_two_grad,
        shift_two_grad,
        up_w_grad,
        up_b_grad,
        down_w_grad,
        down_b_grad,
    )
    return (input_grad, grads)


def body(
    tokens,
    segment_ids,
    norm1_gain,
    norm1_shift,
    qkv_weight,
    qv_bias,
    out_weight,
    out_bias,
    norm2_gain,
    norm2_shift,
    fc1_weight,
    fc1_bias,
    fc2_weight,
    fc2_bias,
    cotangent,
):
    stacked = (
        norm1_gain,
        norm1_shift,
        qkv_weight,
        qv_bias,
        out_weight,
        out_bias,
        norm2_gain,
        norm2_shift,
        fc1_weight,
        fc1_bias,
        fc2_weight,
        fc2_bias,
    )
    batch_rows, seq_len = segment_ids.shape
    layer_count = norm1_gain.shape[0]
    grad_scale = float(batch_rows * seq_len * lax.axis_size("dp")) ** (-0.5)
    same_doc = segment_ids[:, :, None] == segment_ids[:, None, :]
    positions = lax.broadcasted_iota(jnp.int32, (seq_len, seq_len), 0)
    earlier = lax.broadcasted_iota(jnp.int32, (seq_len, seq_len), 1) <= positions
    allowed = (same_doc & earlier[None])[:, None]
    hidden = tokens.astype(jnp.float32)
    saved_list = []
    for layer_idx in range(layer_count):
        params = tuple((member[layer_idx] for member in stacked))
        hidden, saved = forward_layer(hidden, allowed, params, batch_rows)
        saved_list.append(saved)
    grad_flow = cotangent.astype(jnp.float32)
    per_layer = [None] * layer_count
    for layer_idx in reversed(range(layer_count)):
        params = tuple((member[layer_idx] for member in stacked))
        grad_flow, grads = backward_layer(
            grad_flow, allowed, params, saved_list[layer_idx], batch_rows
        )
        grads = tuple((member[None] for member in grads))
        per_layer[layer_idx] = grads
    joined = tuple(
        (
            jnp.concatenate([layer_part[position] for layer_part in per_layer], axis=0)
            for position in range(12)
        )
    )
    totals = sum_blocks(joined)
    totals = tuple((member * grad_scale for member in totals))
    return (
        hidden,
        grad_flow,
        totals[0],
        totals[1],
        totals[2],
        totals[3],
        totals[4],
        totals[5],
        totals[6],
        totals[7],
        totals[8],
        totals[9],
        totals[10],
        totals[11],
    )


def solution(mesh):
    return jax.shard_map(
        body,
        mesh=mesh,
        in_specs=(
            P("dp", None),
            P("dp", None),
            P(),
            P(),
            P(None, None, "tensor"),
            P(None, "tensor", None),
            P(None, "tensor", None),
            P(),
            P(),
            P(),
            P(None, None, "tensor"),
            P(None, "tensor"),
            P(None, "tensor", None),
            P(),
            P("dp", None),
        ),
        out_specs=(
            P("dp", None),
            P("dp", None),
            P(None, "dp"),
            P(None, "dp"),
            P(None, "dp", "tensor"),
            P(None, "tensor", "dp"),
            P(None, "tensor", "dp"),
            P(None, "dp"),
            P(None, "dp"),
            P(None, "dp"),
            P(None, "dp", "tensor"),
            P(None, ("tensor", "dp")),
            P(None, "tensor", "dp"),
            P(None, "dp"),
        ),
        check_vma=False,
    )
```

profile of v0, /device:TPU:0, one launch (start us, length us, event | category | flops | bytes accessed | tf_op | source)
XLA Modules:
  0.0 1322.6 jit_solution(4329592551355744151)
XLA Ops:
  9.5 1.6 fusion.25
  17.2 1.4 convolution_convert_fusion.11
  20.3 37.6 %all-reduce.13.cloned.1.call-done = bf16[584,768]{1,0:T(8,128)(2,1)} async-done(((bf16[584,768]{1,0:T(8,128)(2,1)}), bf16[584,768]{1,0:T(8,128)(2,1)}) %all-reduce.13.cloned.1.call-update) | async-done | bytes 897040 | tf_op jit(solution)/shard_map/psum | solution.py:40
  58.0 1.7 fusion.78
  62.8 2.2 convolution_convert_fusion.6
  66.2 34.4 %all-reduce.15.cloned.1.call-done = bf16[584,768]{1,0:T(8,128)(2,1)} async-done(((bf16[584,768]{1,0:T(8,128)(2,1)}), bf16[584,768]{1,0:T(8,128)(2,1)}) %all-reduce.15.cloned.1.call-update) | async-done | bytes 897040 | tf_op jit(solution)/shard_map/psum | solution.py:40
  100.6 2.0 fusion.141
  103.0 1.4 copy-done.31
  108.7 1.4 convolution_convert_fusion.10
  111.6 35.6 %all-reduce.17.cloned.1.call-done = bf16[584,768]{1,0:T(8,128)(2,1)} async-done(((bf16[584,768]{1,0:T(8,128)(2,1)}), bf16[584,768]{1,0:T(8,128)(2,1)}) %all-reduce.17.cloned.1.call-update) | async-done | bytes 897040 | tf_op jit(solution)/shard_map/psum | solution.py:40
  147.3 2.2 fusion.140
  151.8 1.7 fusion.146
  154.5 1.8 convolution_convert_fusion.3
  156.6 35.4 %all-reduce.19.cloned.1.call-done = bf16[584,768]{1,0:T(8,128)(2,1)} async-done(((bf16[584,768]{1,0:T(8,128)(2,1)}), bf16[584,768]{1,0:T(8,128)(2,1)}) %all-reduce.19.cloned.1.call-update) | async-done | bytes 897040 | tf_op jit(solution)/shard_map/psum | solution.py:44
  192.0 2.2 fusion.47
  194.3 2.4 fusion.139
  198.5 1.4 bitcast_reduce_fusion
  200.0 1.9 multiply_convert_fusion.1
  205.0 1.9 convolution_convert_fusion.2
  206.9 35.6 %all-reduce.21.cloned.1.call-done = bf16[584,768]{1,0:T(8,128)(2,1)} async-done(((bf16[584,768]{1,0:T(8,128)(2,1)}), bf16[584,768]{1,0:T(8,128)(2,1)}) %all-reduce.21.cloned.1.call-update) | async-done | bytes 897040 | tf_op jit(solution)/shard_map/psum | solution.py:44
  242.5 3.4 fusion.48
  245.9 2.9 fusion.135
  248.9 2.3 fusion.147
  252.1 1.8 convolution_convert_fusion.1
  254.3 4.0 convolution_convert_fusion.4
  258.3 31.4 %all-reduce.23.cloned.1.call-done = bf16[584,768]{1,0:T(8,128)(2,1)} async-done(((bf16[584,768]{1,0:T(8,128)(2,1)}), bf16[584,768]{1,0:T(8,128)(2,1)}) %all-reduce.23.cloned.1.call-update) | async-done | bytes 897040 | tf_op jit(solution)/shard_map/psum | solution.py:44
  289.6 3.2 fusion.53
  292.9 3.2 fusion.137
  296.8 2.0 bitcast_reduce_fusion.2
  298.9 1.9 multiply_convert_fusion
  304.5 1.8 convolution_convert_fusion
  309.4 2.0 convolution_bitcast_fusion.8
  312.7 1.7 copy.101
  319.6 1.7 copy.99
  321.3 2.8 convolution_bitcast_fusion.9
  331.1 22.6 %all-reduce.27.cloned.1.call-done = (bf16[584,768]{1,0:T(8,128)(2,1)}, bf16[584,768]{1,0:T(8,128)(2,1)}) async-done(((bf16[584,768]{1,0:T(8,128)(2,1)}, bf16[584,768]{1,0:T(8,128)(2,1)}), (bf16[584,768]{1,0:T(8,128)(2,1)}, bf16[584,768]{1,0:T(8,128)(2,1)})) %all-reduce.27.cloned.1.call-update) | async-done | bytes 1794064 | tf_op jit(solution)/shard_map/psum | solution.py:40
  353.7 2.1 fusion.54
  358.1 2.2 pad_maximum_fusion.3
  360.4 3.4 copy.91
  363.8 3.2 reshape.521
  367.2 3.3 convolution_bitcast_fusion
  370.5 2.3 convolution_bitcast_fusion.4
  372.8 1.5 convolution_bitcast_fusion.1
  374.3 2.5 pad_maximum_fusion.1
  376.7 8.3 copy.69
  386.5 2.0 pad_maximum_fusion.2
  388.5 7.5 copy.68
  396.7 2.8 convolution_bitcast_fusion.2
  399.5 1.6 convolution_bitcast_fusion.3
  401.1 2.5 pad_maximum_fusion
  405.5 13.2 reduce-scatter.47.cloned.1.call-done
  419.6 63.2 %reduce-scatter.45.cloned.1.call-done = f32[96,2]{1,0:T(8,128)} async-done(((f32[768,2]{1,0:T(8,128)}), f32[96,2]{1,0:T(8,128)}) %reduce-scatter.45.cloned.1.call-update) | async-done | bytes 784
  484.8 62.5 %reduce-scatter.35.cloned.1.call-done = f32[16,6]{1,0:T(8,128)} async-done(((f32[128,6]{1,0:T(8,128)}), f32[16,6]{1,0:T(8,128)}) %reduce-scatter.35.cloned.1.call-update) | async-done | bytes 400
  548.7 62.6 %reduce-scatter.39.cloned.1.call-done = f32[96,2]{1,0:T(8,128)} async-done(((f32[768,2]{1,0:T(8,128)}), f32[96,2]{1,0:T(8,128)}) %reduce-scatter.39.cloned.1.call-update) | async-done | bytes 784
  612.2 63.0 %reduce-scatter.43.cloned.1.call-done = f32[96,2]{1,0:T(8,128)} async-done(((f32[768,2]{1,0:T(8,128)}), f32[96,2]{1,0:T(8,128)}) %reduce-scatter.43.cloned.1.call-update) | async-done | bytes 784
  676.1 63.2 %reduce-scatter.41.cloned.1.call-done = f32[96,2]{1,0:T(8,128)} async-done(((f32[768,2]{1,0:T(8,128)}), f32[96,2]{1,0:T(8,128)}) %reduce-scatter.41.cloned.1.call-update) | async-done | bytes 784
  741.9 2.8 add_add_fusion
  744.7 1.9 fusion.24
  746.6 57.3 %reduce-scatter.33.cloned.1.call-done = f32[96,2]{1,0:T(8,128)} async-done(((f32[768,2]{1,0:T(8,128)}), f32[96,2]{1,0:T(8,128)}) %reduce-scatter.33.cloned.1.call-update) | async-done | bytes 784
  804.7 63.6 %reduce-scatter.31.cloned.1.call-done = f32[96,2]{1,0:T(8,128)} async-done(((f32[768,2]{1,0:T(8,128)}), f32[96,2]{1,0:T(8,128)}) %reduce-scatter.31.cloned.1.call-update) | async-done | bytes 784
  870.2 64.8 %reduce-scatter.37.cloned.1.call-done = f32[96,384]{1,0:T(8,128)} async-done(((f32[768,384]{1,0:T(8,128)}), f32[96,384]{1,0:T(8,128)}) %reduce-scatter.37.cloned.1.call-update) | async-done | bytes 147472
  936.9 278.9 %all-reduce.25.cloned.1.call-done = (f32[2,768,576]{2,0,1:T(2,128)}, f32[2,768,768]{1,0,2:T(2,128)}) async-done(((f32[2,768,576]{2,0,1:T(2,128)}, f32[2,768,768]{1,0,2:T(2,128)}), (f32[2,768,576]{2,0,1:T(2,128)}, f32[2,768,768]{1,0,2:T(2,128)})) %all-reduce.25.cloned.1.call-update) | async-done | bytes 8257552
  1220.2 93.5 %reduce-scatter.29.cloned.1.call-done = f32[2,96,768]{2,1,0:T(8,128)} async-done(((f32[2,768,768]{2,1,0:T(8,128)}), f32[2,96,768]{2,1,0:T(8,128)}) %reduce-scatter.29.cloned.1.call-update) | async-done | bytes 589840 | tf_op jit(solution)/shard_map/reduce_scatter | solution.py:57
  1313.7 1.9 broadcast_multiply_fusion
  (339 shorter events, 74.2 us)
Async XLA Ops:
  7.2 4.0 copy-start.74
  7.2 4.2 copy-start.27
  7.2 50.8 %all-reduce.13.cloned.1.call-start = ((), (), s32[]{:S(2)}) async-start(), calls=%async_computation.10 | async-start | bytes 1794048 | tf_op jit(solution)/shard_map/psum | solution.py:40
  12.5 90.4 %copy-start.68 = (f32[768]{0:T(1024)}, f32[768]{0:T(1024)S(1)}, u32[]{:S(2)}) copy-start(f32[768]{0:T(1024)S(1)} %get-tuple-element.84) | copy-start | bytes 9220
  12.6 233.3 %copy-start.44 = (f32[768]{0:T(1024)}, f32[768]{0:T(1024)S(1)}, u32[]{:S(2)}) copy-start(f32[768]{0:T(1024)S(1)} %get-tuple-element.128) | copy-start | bytes 9220
  20.1 80.5 %all-reduce.15.cloned.1.call-start = ((), (), s32[]{:S(2)}) async-start(), calls=%async_computation.11 | async-start | bytes 1794048 | tf_op jit(solution)/shard_map/psum | solution.py:40
  20.2 228.6 %copy-start.70 = (f32[768]{0:T(1024)}, f32[768]{0:T(1024)S(1)}, u32[]{:S(2)}) copy-start(f32[768]{0:T(1024)S(1)} %get-tuple-element.75) | copy-start | bytes 9220
  20.3 234.0 %copy-start.72 = (f32[768]{0:T(1024)}, f32[768]{0:T(1024)S(1)}, u32[]{:S(2)}) copy-start(f32[768]{0:T(1024)S(1)} %get-tuple-element.74) | copy-start | bytes 9220
  20.3 39.9 %copy-start.64 = (f32[768]{0:T(1024)}, f32[768]{0:T(1024)S(1)}, u32[]{:S(2)}) copy-start(f32[768]{0:T(1024)S(1)} %get-tuple-element.79) | copy-start | bytes 9220
  20.3 129.5 %copy-start.66 = (f32[768]{0:T(1024)}, f32[768]{0:T(1024)S(1)}, u32[]{:S(2)}) copy-start(f32[768]{0:T(1024)S(1)} %get-tuple-element.78) | copy-start | bytes 9220
  20.3 173.9 %copy-start.36 = (f32[768]{0:T(1024)}, f32[768]{0:T(1024)S(1)}, u32[]{:S(2)}) copy-start(f32[768]{0:T(1024)S(1)} %get-tuple-element.130) | copy-start | bytes 9220
  60.2 232.7 %copy-start.40 = (f32[584]{0:T(1024)}, f32[584]{0:T(1024)S(1)}, u32[]{:S(2)}) copy-start(f32[584]{0:T(1024)S(1)} %add_rsqrt_fusion.2) | copy-start | bytes 7012
  65.0 82.3 %all-reduce.17.cloned.1.call-start = ((), (), s32[]{:S(2)}) async-start(), calls=%async_computation.12 | async-start | bytes 1794048 | tf_op jit(solution)/shard_map/psum | solution.py:40
  102.6 2.9 copy-start.1
  103.0 142.9 %copy-start.46 = (f32[584]{0:T(1024)}, f32[584]{0:T(1024)S(1)}, u32[]{:S(2)}) copy-start(f32[584]{0:T(1024)S(1)} %add_rsqrt_fusion.1) | copy-start | bytes 7012
  110.2 37.1 %copy-start.24 = (bf16[3,64,584]{2,1,0:T(8,128)(2,1)}, bf16[3,64,584]{2,1,0:T(8,128)(2,1)S(1)}, u32[]{:S(2)}) copy-start(bf16[3,64,584]{2,1,0:T(8,128)(2,1)S(1)} %convolution_convert_fusion.10) | copy-start | bytes 672772
  111.6 80.4 %all-reduce.19.cloned.1.call-start = ((), (), s32[]{:S(2)}) async-start(), calls=%async_computation.13 | async-start | bytes 1794048 | tf_op jit(solution)/shard_map/psum | solution.py:44
  149.8 44.4 %copy-start.42 = (f32[584]{0:T(1024)}, f32[584]{0:T(1024)S(1)}, u32[]{:S(2)}) copy-start(f32[584]{0:T(1024)S(1)} %add_rsqrt_fusion) | copy-start | bytes 7012
  156.3 86.2 %all-reduce.21.cloned.1.call-start = ((), (), s32[]{:S(2)}) async-start(), calls=%async_computation.14 | async-start | bytes 1794048 | tf_op jit(solution)/shard_map/psum | solution.py:44
  192.0 6.5 slice-start.2
  194.2 3.6 copy-start.22
  194.3 4.2 slice-start.3
  206.9 82.7 %all-reduce.23.cloned.1.call-start = ((), (), s32[]{:S(2)}) async-start(), calls=%async_computation.15 | async-start | bytes 1794048 | tf_op jit(solution)/shard_map/psum | solution.py:44
  242.5 3.4 copy-start.2
  242.5 3.4 copy-start.15
  245.9 2.9 copy-start.81
  245.9 2.9 copy-start.85
  248.9 3.3 copy-start.78
  254.0 99.7 %all-reduce.27.cloned.1.call-start = ((), (), s32[]{:S(2)}) async-start(), calls=%async_computation.27 | async-start | bytes 3588096 | tf_op jit(solution)/shard_map/psum | solution.py:40
  289.6 3.2 copy-start.8
  289.6 7.1 slice-start
  292.9 3.3 copy-start.23
  292.9 3.9 slice-start.1
  306.3 112.4 %reduce-scatter.47.cloned.1.call-start = ((), (), s32[]{:S(2)}) async-start(), calls=%async_computation.25 | async-start | bytes 442368
  315.7 167.1 %reduce-scatter.45.cloned.1.call-start = ((), (), s32[]{:S(2)}) async-start(), calls=%async_computation.24 | async-start | bytes 442368
  321.2 226.0 %reduce-scatter.35.cloned.1.call-start = ((), (), s32[]{:S(2)}) async-start(), calls=%async_computation.19 | async-start | bytes 73728
  321.3 2.8 copy-start.54
  321.3 2.9 copy-start.53
  321.3 2.9 copy-start.48
  324.1 5.9 copy-start.51
  324.1 29.6 %copy-start.39 = (f32[584]{0:T(1024)S(1)}, f32[584]{0:T(1024)}, u32[]{:S(2)}) copy-start(f32[584]{0:T(1024)} %copy-done.38) | copy-start | bytes 7012
  325.1 286.2 %reduce-scatter.39.cloned.1.call-start = ((), (), s32[]{:S(2)}) async-start(), calls=%async_computation.21 | async-start | bytes 442368
  327.5 28.3 %copy-start.52 = (f32[1,768]{1,0:T(1,128)S(1)}, f32[1,768]{1,0:T(1,128)}, u32[]{:S(2)}) copy-start(f32[1,768]{1,0:T(1,128)} %broadcast_in_dim.131) | copy-start | bytes 9220
  327.5 347.7 %reduce-scatter.43.cloned.1.call-start = ((), (), s32[]{:S(2)}) async-start(), calls=%async_computation.23 | async-start | bytes 442368
  329.9 26.9 %copy-start.50 = (f32[1,768]{1,0:T(1,128)S(1)}, f32[1,768]{1,0:T(1,128)}, u32[]{:S(2)}) copy-start(f32[1,768]{1,0:T(1,128)} %broadcast_in_dim.129) | copy-start | bytes 9220
  330.0 409.3 %reduce-scatter.41.cloned.1.call-start = ((), (), s32[]{:S(2)}) async-start(), calls=%async_computation.22 | async-start | bytes 442368
  331.0 472.8 %reduce-scatter.33.cloned.1.call-start = ((), (), s32[]{:S(2)}) async-start(), calls=%async_computation.18 | async-start | bytes 442368
  356.8 511.5 %reduce-scatter.31.cloned.1.call-start = ((), (), s32[]{:S(2)}) async-start(), calls=%async_computation.17 | async-start | bytes 442368
  357.8 577.2 %reduce-scatter.37.cloned.1.call-start = ((), (), s32[]{:S(2)}) async-start(), calls=%async_computation.20 | async-start | bytes 1327104
  363.8 3.4 copy-start.73
  367.1 3.4 copy-start.33
  367.1 3.4 copy-start.45
  367.1 3.4 copy-start.47
  367.1 3.4 copy-start.69
  367.1 848.7 %all-reduce.25.cloned.1.call-start = ((), (), s32[]{:S(2)}) async-start(), calls=%async_computation.26 | async-start | bytes 17301504
  367.2 3.3 copy-start.3
  376.7 8.3 copy-start.35
  376.7 8.3 copy-start.63
  396.0 3.5 copy-start.41
  396.0 3.5 copy-start.65
  396.0 917.6 %reduce-scatter.29.cloned.1.call-start = ((), (), s32[]{:S(2)}) async-start(), calls=%async_computation.16 | async-start | bytes 5308416 | tf_op jit(solution)/shard_map/reduce_scatter | solution.py:57
  396.7 2.8 copy-start.9
  396.7 2.8 copy-start.89
  403.6 338.2 %copy-start.49 = (f32[768]{0:T(1024)S(1)}, f32[768]{0:T(1024)}, u32[]{:S(2)}) copy-start(f32[768]{0:T(1024)} %get-tuple-element.72) | copy-start | bytes 9220
  (48 other events, 83.0 us)
Sparse Core Ops, SparseCore 0:
  20.2 37.7 all-reduce.12
  65.1 35.4 all-reduce.14
  111.7 35.5 all-reduce.16
  156.5 35.4 all-reduce.18
  207.0 35.4 all-reduce.20
  254.1 35.4 all-reduce.22
  306.5 47.1 all-reduce.26
  357.3 61.3 reduce-scatter.46
  422.3 60.3 reduce-scatter.44
  487.0 60.2 reduce-scatter.34
  550.9 60.3 reduce-scatter.38
  614.8 60.3 reduce-scatter.42
  678.8 60.4 reduce-scatter.40
  743.3 60.4 reduce-scatter.32
  807.8 60.3 reduce-scatter.30
  871.9 63.1 reduce-scatter.36
  939.4 276.4 all-reduce.24
  1219.4 94.2 reduce-scatter.28
where the time goes:
time: 1330 us; the launch traced here: 1320 us
  waiting for transfers between devices  1120 us (84%)
  local copies, waits for them, and re-layouts  67 us (5%)
  other arithmetic  59.5 us (4%)
  matrix products  58.7 us (4%)
  between operations  16.4 us (1%)
    unnamed x28, waiting for transfers between devices  793 us
    psum x4, waiting for transfers between devices, branch_total(): lax.psum(partial_sum.astype(jnp.bfloat16), 'tensor').astype(jnp.float32)  130 us
    psum x3, waiting for transfers between devices, input_total(): lax.psum(partial_sum.astype(jnp.bfloat16), 'tensor').astype(jnp.float32)  102 us
    reduce_scatter x1, waiting for transfers between devices, sum_blocks(): lax.psum_scatter(grads[8], 'dp', scatter_dimension=1, tiled=True)  93.5 us
    unnamed x215, local copies, waits for them, and re-layouts  40.2 us
  transfers between devices with their start and end apart: 18, of which 18 were waited for; matrix products, arithmetic and copies ran while one was open for 8% of the time, Pallas kernels for 0%

commit v1 on v0

--- a/solution.py
+++ b/solution.py
@@ -1,6 +1,10 @@
+import functools
+
 import jax
 import jax.numpy as jnp
 from jax import lax
+from jax.experimental import pallas as pl
+from jax.experimental.pallas import tpu as pltpu
 from jax.sharding import PartitionSpec as P
 
 NORM_EPS = 1e-05
@@ -36,29 +40,106 @@
     return (gelu_out, gelu_slope)
 
 
-def branch_total(partial_sum):
-    return lax.psum(partial_sum.astype(jnp.bfloat16), "tensor").astype(jnp.float32)
-
-
-def input_total(partial_sum):
-    return lax.psum(partial_sum.astype(jnp.bfloat16), "tensor").astype(jnp.float32)
-
-
-def sum_blocks(grads):
-    return (
-        lax.psum_scatter(grads[0], "dp", scatter_dimension=1, tiled=True),
-        lax.psum_scatter(grads[1], "dp", scatter_dimension=1, tiled=True),
-        lax.psum_scatter(grads[2], "dp", scatter_dimension=1, tiled=True),
-        lax.psum_scatter(grads[3], "dp", scatter_dimension=2, tiled=True),
-        lax.psum_scatter(grads[4], "dp", scatter_dimension=2, tiled=True),
-        lax.psum_scatter(grads[5], "dp", scatter_dimension=1, tiled=True),
-        lax.psum_scatter(grads[6], "dp", scatter_dimension=1, tiled=True),
-        lax.psum_scatter(grads[7], "dp", scatter_dimension=1, tiled=True),
-        lax.psum_scatter(grads[8], "dp", scatter_dimension=1, tiled=True),
-        lax.psum_scatter(grads[9], "dp", scatter_dimension=1, tiled=True),
-        lax.psum_scatter(grads[10], "dp", scatter_dimension=2, tiled=True),
-        lax.psum_scatter(grads[11], "dp", scatter_dimension=1, tiled=True),
-    )
+MESH = pl.DeviceIdType.MESH
+CHUNK = 128
+
+
+def total_kernel(transposed, x_ref, w_ref, out_ref, own, near_out, near_in, far_out, far_in,
+                 near_send, near_recv, far_send, far_recv, back_send, back_recv):
+    here = lax.axis_index("tensor")
+    core = lax.rem(here, 2)
+    near = here + 1 - 2 * core
+    far = lax.rem(here + 2, 4)
+    barrier = pltpu.get_barrier_semaphore()
+    for other in (near, far):
+        pl.semaphore_signal(barrier, inc=1, device_id={"tensor": other}, device_id_type=MESH)
+
+    half = out_ref.shape[1] // 2
+    count = half // CHUNK
+
+    def part(side, j):
+        start = pl.multiple_of(side * half + j * CHUNK, CHUNK)
+        if transposed:
+            return lax.dot_general(
+                x_ref[...], w_ref[pl.ds(start, CHUNK), :], (((1,), (1,)), ((), ())),
+                preferred_element_type=jnp.float32,
+            )
+        return jnp.dot(x_ref[...], w_ref[:, pl.ds(start, CHUNK)], preferred_element_type=jnp.float32)
+
+    def copy(src, dst, send, recv, other):
+        return pltpu.make_async_remote_copy(
+            src_ref=src, dst_ref=dst, send_sem=send, recv_sem=recv,
+            device_id={"tensor": other}, device_id_type=MESH,
+        )
+
+    first = [copy(near_out.at[j], near_in.at[j], near_send.at[j], near_recv.at[j], near) for j in range(count)]
+    second = [copy(far_out.at[j], far_in.at[j], far_send.at[j], far_recv.at[j], far) for j in range(count)]
+
+    def back_copy(j):
+        columns = pl.ds(pl.multiple_of(core * half + j * CHUNK, CHUNK), CHUNK)
+        return copy(out_ref.at[:, columns], out_ref.at[:, columns], back_send.at[j], back_recv.at[j], near)
+
+    third = [back_copy(j) for j in range(count)]
+
+    near_out[0] = part(1 - core, 0).astype(jnp.bfloat16)
+    pl.semaphore_wait(barrier, 2)
+    first[0].start()
+    own[0] = part(core, 0)
+    for j in range(count):
+        if j + 1 < count:
+            near_out[j + 1] = part(1 - core, j + 1).astype(jnp.bfloat16)
+            first[j + 1].start()
+            own[j + 1] = part(core, j + 1)
+        first[j].wait_recv()
+        far_out[j] = (own[j] + near_in[j].astype(jnp.float32)).astype(jnp.bfloat16)
+        second[j].start()
+    for j in range(count):
+        second[j].wait_recv()
+        columns = pl.ds(pl.multiple_of(core * half + j * CHUNK, CHUNK), CHUNK)
+        out_ref[:, columns] = (
+            far_out[j].astype(jnp.float32) + far_in[j].astype(jnp.float32)
+        ).astype(jnp.bfloat16)
+        third[j].start()
+    for j in range(count):
+        first[j].wait_send()
+        second[j].wait_send()
+        third[j].wait()
+
+
+def group_total(x, w, transposed, collective_id):
+    rows = x.shape[0]
+    columns = w.shape[0] if transposed else w.shape[1]
+    count = columns // 2 // CHUNK
+    vmem = pl.BlockSpec(memory_space=pltpu.VMEM)
+    slot = pltpu.VMEM((count, rows, CHUNK), jnp.bfloat16)
+    return pl.pallas_call(
+        functools.partial(total_kernel, transposed),
+        out_shape=jax.ShapeDtypeStruct((rows, columns), jnp.bfloat16),
+        in_specs=[vmem, vmem],
+        out_specs=vmem,
+        scratch_shapes=[pltpu.VMEM((count, rows, CHUNK), jnp.float32), slot, slot, slot, slot]
+        + [pltpu.SemaphoreType.DMA((count,))] * 6,
+        compiler_params=pltpu.CompilerParams(
+            collective_id=collective_id, has_side_effects=True, vmem_limit_bytes=32 * 2**20
+        ),
+        cost_estimate=pl.CostEstimate(
+            flops=2 * rows * columns * x.shape[1], bytes_accessed=rows * columns * 8, transcendentals=0
+        ),
+    )(x, w).astype(jnp.float32)
+
+
+def spread(grad, dimension):
+    return lax.psum_scatter(
+        grad.astype(jnp.bfloat16), "dp", scatter_dimension=dimension, tiled=True
+    ).astype(jnp.float32)
+
+
+SPLIT = (0, 0, 0, 1, 1, 0, 0, 0, 0, 0, 1, 0)
+
+
+def sum_layer(grads):
+    return tuple(spread(g, d) if g.ndim > 1 and g.shape[0] > 8 else
+                 lax.psum_scatter(g, "dp", scatter_dimension=d, tiled=True) for g, d in zip(grads, SPLIT))
 
 
 def attend_scores(queries, key_vecs, allowed):
@@ -103,7 +184,7 @@
     mixed_heads = mixed_heads.astype(jnp.bfloat16).reshape(tok_count, local_heads * head_size)
     after_attn = (
         hidden
-        + branch_total(jnp.dot(mixed_heads, out_w, preferred_element_type=jnp.float32))
+        + group_total(mixed_heads, out_w, False, 0)
         + out_b
     )
     middle, normal_two, inverse_two = layer_norm(after_attn, gain_two, shift_two)
@@ -113,7 +194,7 @@
     gelu_b = gelu_out.astype(jnp.bfloat16)
     block_out = (
         after_attn
-        + branch_total(jnp.dot(gelu_b, down_w, preferred_element_type=jnp.float32))
+        + group_total(gelu_b, down_w, False, 1)
         + down_b
     )
     saved = (
@@ -176,9 +257,7 @@
     up_b_grad = jnp.sum(pre_grad, axis=0)
     pre_grad_b = pre_grad.astype(jnp.bfloat16)
     up_w_grad = jnp.einsum("nd,nf->df", mid_b, pre_grad_b, preferred_element_type=jnp.float32)
-    mid_grad = input_total(
-        jnp.einsum("nf,df->nd", pre_grad_b, up_w, preferred_element_type=jnp.float32)
-    )
+    mid_grad = group_total(pre_grad_b, up_w, True, 2)
     gain_two_grad = jnp.sum(mid_grad * normal_two, axis=0)
     shift_two_grad = jnp.sum(mid_grad, axis=0)
     resid_grad = grad_out + norm_backward(mid_grad, normal_two, inverse_two, gain_two)
@@ -214,9 +293,7 @@
     proj_grad = jnp.stack([query_grad, key_grad, value_grad], axis=3).astype(jnp.bfloat16)
     proj_grad = proj_grad.reshape(tok_count, local_heads * 3 * head_size)
     qkv_w_grad = jnp.einsum("nd,nc->dc", normed_b, proj_grad, preferred_element_type=jnp.float32)
-    normed_grad = input_total(
-        jnp.einsum("nc,dc->nd", proj_grad, qkv_w, preferred_element_type=jnp.float32)
-    )
+    normed_grad = group_total(proj_grad, qkv_w, True, 3)
     gain_one_grad = jnp.sum(normed_grad * normal_one, axis=0)
     shift_one_grad = jnp.sum(normed_grad, axis=0)
     input_grad = resid_grad + norm_backward(normed_grad, normal_one, inverse_one, gain_one)
@@ -271,49 +348,39 @@
     batch_rows, seq_len = segment_ids.shape
     layer_count = norm1_gain.shape[0]
     grad_scale = float(batch_rows * seq_len * lax.axis_size("dp")) ** (-0.5)
+    padded = -(-seq_len // 16) * 16
+    extra = padded - seq_len
+    segment_ids = jnp.pad(segment_ids, ((0, 0), (0, extra)), constant_values=-1)
     same_doc = segment_ids[:, :, None] == segment_ids[:, None, :]
-    positions = lax.broadcasted_iota(jnp.int32, (seq_len, seq_len), 0)
-    earlier = lax.broadcasted_iota(jnp.int32, (seq_len, seq_len), 1) <= positions
+    positions = lax.broadcasted_iota(jnp.int32, (padded, padded), 0)
+    earlier = lax.broadcasted_iota(jnp.int32, (padded, padded), 1) <= positions
     allowed = (same_doc & earlier[None])[:, None]
-    hidden = tokens.astype(jnp.float32)
+
+    def widen(rows):
+        rows = rows.astype(jnp.float32).reshape(batch_rows, seq_len, -1)
+        return jnp.pad(rows, ((0, 0), (0, extra), (0, 0))).reshape(batch_rows * padded, -1)
+
+    def narrow(rows):
+        return rows.reshape(batch_rows, padded, -1)[:, :seq_len].reshape(batch_rows * seq_len, -1)
+
+    hidden = widen(tokens)
     saved_list = []
     for layer_idx in range(layer_count):
         params = tuple((member[layer_idx] for member in stacked))
         hidden, saved = forward_layer(hidden, allowed, params, batch_rows)
         saved_list.append(saved)
-    grad_flow = cotangent.astype(jnp.float32)
+    grad_flow = widen(cotangent)
     per_layer = [None] * layer_count
     for layer_idx in reversed(range(layer_count)):
         params = tuple((member[layer_idx] for member in stacked))
         grad_flow, grads = backward_layer(
             grad_flow, allowed, params, saved_list[layer_idx], batch_rows
         )
-        grads = tuple((member[None] for member in grads))
-        per_layer[layer_idx] = grads
-    joined = tuple(
-        (
-            jnp.concatenate([layer_part[position] for layer_part in per_layer], axis=0)
-            for position in range(12)
-        )
-    )
-    totals = sum_blocks(joined)
-    totals = tuple((member * grad_scale for member in totals))
-    return (
-        hidden,
-        grad_flow,
-        totals[0],
-        totals[1],
-        totals[2],
-        totals[3],
-        totals[4],
-        totals[5],
-        totals[6],
-        totals[7],
-        totals[8],
-        totals[9],
-        totals[10],
-        totals[11],
-    )
+        per_layer[layer_idx] = sum_layer(grads)
+    totals = tuple(
+        jnp.stack([part[i] for part in per_layer], axis=0) * grad_scale for i in range(12)
+    )
+    return (narrow(hidden), narrow(grad_flow)) + totals
 
 
 def solution(mesh):

time: 1330 us -> 816 us (0.61)
  waiting for transfers between devices: 1120 us -> 484 us
  Pallas kernels: 0 us -> 124 us
  blocking collectives: 0 us -> 37.9 us
  other arithmetic: 59.5 us -> 37.3 us
  local copies, waits for them, and re-layouts: 67 us -> 46.1 us
    unnamed x28 -> x14, waiting for transfers between devices: 793 us -> 91.9 us
    reduce_scatter x1 -> x6, waiting for transfers between devices: 93.5 us -> 392 us  [spread(): lax.psum_scatter(grad.astype(jnp.bfloat16), 'dp', scatter_dimension=dimen...]
    psum x7 -> x0, waiting for transfers between devices: 233 us -> none  [the longest x4 130 us: branch_total(): lax.psum(partial_sum.astype(jnp.bfloat16), 'tensor').astype(jnp.float32)]
    pallas_call x0 -> x8, Pallas kernels: none -> 124 us  [group_total(): pl.pallas_call(functools.partial(total_kernel, transposed), out_shape=jax...]
    unnamed x0 -> x1, blocking collectives: none -> 37.9 us
    dot_general x8 -> x0, matrix products: 16.3 us -> none  [the longest x2 6.17 us: forward_layer(): jnp.dot(gelu_b, down_w, preferred_element_type=jnp.float32)]
    concatenate x2 -> x0, local copies, waits for them, and re-layouts: 15.8 us -> none  [body(): jnp.concatenate([layer_part[position] for layer_part in per_layer], axis=0)]
    unnamed x215 -> x275, local copies, waits for them, and re-layouts: 40.2 us -> 28.5 us
  transfers between devices with their start and end apart: 18 -> 10, of which waited for: 18 -> 8; matrix products, arithmetic and copies ran while one was open for 8% -> 9% of each run, Pallas kernels for 0% -> 6%
where the time goes in v1:
time: 816 us; the launch traced here: 806 us
  waiting for transfers between devices  484 us (59%)
  Pallas kernels  124 us (15%)
  matrix products  58 us (7%)
  local copies, waits for them, and re-layouts  46.1 us (6%)
  blocking collectives  37.9 us (5%)
  other arithmetic  37.3 us (5%)
  between operations  17 us (2%)
    reduce_scatter x6, waiting for transfers between devices, spread(): lax.psum_scatter(grad.astype(jnp.bfloat16), 'dp', scatter_dimension=dimen...  392 us
    pallas_call x8, Pallas kernels, group_total(): pl.pallas_call(functools.partial(total_kernel, transposed), out_shape=jax...  124 us
    unnamed x14, waiting for transfers between devices  91.9 us
    unnamed x1, blocking collectives  37.9 us
    unnamed x275, local copies, waits for them, and re-layouts  28.5 us
  transfers between devices with their start and end apart: 10, of which 8 were waited for; matrix products, arithmetic and copies ran while one was open for 9% of the time, Pallas kernels for 6%

profile of v1, /device:TPU:0, one launch (start us, length us, event | category | flops | bytes accessed | tf_op | source)
XLA Modules:
  0.0 805.6 jit_solution(209377804577835691)
XLA Ops:
  8.8 1.4 convert_reduce_fusion.4
  10.2 1.6 fusion.27
  15.7 1.2 slice_bitcast_fusion.5
  16.9 1.2 copy-done.48
  23.8 1.4 convolution_convert_fusion.12
  28.2 16.5 %shard_map.254 = bf16[592,768]{1,0:T(8,128)(2,1)S(1)} custom-call(bf16[592,192]{1,0:T(8,128)(2,1)S(1)} %copy-done.3, bf16[192,768]{1,0:T(8,128)(2,1)S(1)} %copy-done.6), custom_call_target="tpu_custom_call" | custom-call | flops 174587904 | bytes 3637248 | tf_op jit(solution)/shard_map/pallas_call | solution.py:115
  44.7 1.7 fusion.70
  47.6 2.7 multiply_convert_fusion.3
  50.3 15.9 %shard_map.255 = bf16[592,768]{1,0:T(8,128)(2,1)S(1)} custom-call(bf16[592,768]{1,0:T(8,128)(2,1)S(1)} %get-tuple-element.135.x_ref, bf16[768,768]{1,0:T(8,128)(2,1)S(1)} %copy-done.1), custom_call_target="tpu_custom_call" | custom-call | flops 698351616 | bytes 3637248 | tf_op jit(solution)/shard_map/pallas_call | solution.py:115
  67.2 1.4 copy-done.35
  72.9 1.4 convolution_convert_fusion.11
  77.2 15.3 %shard_map.256 = bf16[592,768]{1,0:T(8,128)(2,1)S(1)} custom-call(bf16[592,192]{1,0:T(8,128)(2,1)S(1)} %copy-done.4, bf16[192,768]{1,0:T(8,128)(2,1)S(1)} %copy-done.5), custom_call_target="tpu_custom_call" | custom-call | flops 174587904 | bytes 3637248 | tf_op jit(solution)/shard_map/pallas_call | solution.py:115
  92.5 2.0 fusion.121
  95.3 1.3 multiply_convert_fusion.2
  97.2 2.3 fusion.124
  99.5 15.3 %shard_map.258 = bf16[592,768]{1,0:T(8,128)(2,1)S(1)} custom-call(bf16[592,768]{1,0:T(8,128)(2,1)S(1)} %get-tuple-element.117.x_ref, bf16[768,768]{1,0:T(8,128)(2,1)S(1)} %copy-done), custom_call_target="tpu_custom_call" | custom-call | flops 698351616 | bytes 3637248 | tf_op jit(solution)/shard_map/pallas_call | solution.py:115
  114.8 1.4 fusion.53
  116.2 15.3 %shard_map.257 = bf16[592,768]{1,0:T(8,128)(2,1)S(1)} custom-call(bf16[592,768]{1,0:T(8,128)(2,1)S(1)} %get-tuple-element.140.x_ref, bf16[768,768]{1,0:T(8,128)(2,1)S(1)} %get-tuple-element.112.w_ref), custom_call_target="tpu_custom_call" | custom-call | flops 698351616 | bytes 3637248 | tf_op jit(solution)/shard_map/pallas_call | solution.py:115
  131.6 3.0 fusion.119
  134.6 2.0 convolution_convert_fusion.10
  136.8 2.0 fusion.127
  138.8 1.8 multiply_convert_fusion.1
  140.7 1.4 copy-done.28
  142.1 1.2 fusion.126
  144.2 1.7 copy.113
  145.9 2.6 fusion.62
  149.7 2.3 copy.82.x_ref
  153.1 15.3 %shard_map.259 = bf16[592,768]{1,0:T(8,128)(2,1)S(1)} custom-call(bf16[592,576]{1,0:T(8,128)(2,1)S(1)} %copy-done.2, bf16[768,576]{1,0:T(8,128)(2,1)S(1)} %bitcast.322), custom_call_target="tpu_custom_call" | custom-call | flops 523763712 | bytes 3637248 | tf_op jit(solution)/shard_map/pallas_call | solution.py:115
  168.4 1.4 fusion.54
  169.9 2.9 fusion.115
  172.9 2.3 fusion.123
  175.2 15.2 %shard_map.260 = bf16[592,768]{1,0:T(8,128)(2,1)S(1)} custom-call(bf16[592,768]{1,0:T(8,128)(2,1)S(1)} %get-tuple-element.115.x_ref, bf16[768,768]{1,0:T(8,128)(2,1)S(1)} %get-tuple-element.110.w_ref), custom_call_target="tpu_custom_call" | custom-call | flops 698351616 | bytes 3637248 | tf_op jit(solution)/shard_map/pallas_call | solution.py:115
  190.5 1.6 fusion.59
  192.1 1.5 fusion.117
  193.6 1.2 copy-done.20
  195.5 2.3 bitcast_reduce_fusion
  197.8 1.9 multiply_convert_fusion
  199.7 1.4 copy-done.27
  202.6 1.9 convolution_convert_fusion.6
  205.6 2.0 convolution_convert_fusion.7
  208.6 3.8 convolution_convert_fusion.4
  212.4 2.6 convolution_bitcast_fusion.2
  216.3 2.3 convolution_convert_fusion.5
  218.8 3.9 convolution_convert_fusion.2
  222.8 3.7 convolution_convert_fusion.3
  226.6 3.4 convolution_convert_fusion
  230.4 3.7 convolution_convert_fusion.1
  235.9 1.5 copy.88.x_ref
  237.5 15.3 %shard_map.261 = bf16[592,768]{1,0:T(8,128)(2,1)S(1)} custom-call(bf16[592,576]{1,0:T(8,128)(2,1)S(1)} %copy.88.x_ref, bf16[768,576]{1,0:T(8,128)(2,1)S(1)} %bitcast.323), custom_call_target="tpu_custom_call" | custom-call | flops 523763712 | bytes 3637248 | tf_op jit(solution)/shard_map/pallas_call | solution.py:115
  255.3 37.9 %all-reduce.17 = (f32[768]{0:T(1024)S(1)}, f32[768]{0:T(1024)S(1)}, f32[768]{0:T(1024)S(1)}, f32[768]{0:T(1024)S(1)}, f32[768]{0:T(1024)S(1)}, /*index=5*/f32[76...) all-reduce(f32[768]{0:T(1024)S(1)} %copy-done.88, ...), channel_id=3, replica_groups=mesh['dp'=8,'tensor'=4] {'dp'}, use_global_device_ids=true, to_apply=%region_25.26.clone | all-reduce | flops 10752 | bytes 86016
  298.3 2.2 fusion.26
  300.4 1.3 slice_bitcast_fusion
  302.6 1.3 slice_bitcast_fusion.1
  306.1 28.5 %reduce-scatter.37.cloned.1.call-done = bf16[96,192]{1,0:T(8,128)(2,1)} async-done(((bf16[768,192]{1,0:T(8,128)(2,1)}), bf16[96,192]{1,0:T(8,128)(2,1)}) %reduce-scatter.37.cloned.1.call-update) | async-done | bytes 36880
  335.5 63.2 %reduce-scatter.35.cloned.1.call-done = bf16[96,192]{1,0:T(8,128)(2,1)} async-done(((bf16[768,192]{1,0:T(8,128)(2,1)}), bf16[96,192]{1,0:T(8,128)(2,1)}) %reduce-scatter.35.cloned.1.call-update) | async-done | bytes 36880
  400.3 64.0 %reduce-scatter.21.cloned.1.call-done = bf16[96,576]{1,0:T(8,128)(2,1)} async-done(((bf16[768,576]{1,0:T(8,128)(2,1)}), bf16[96,576]{1,0:T(8,128)(2,1)}) %reduce-scatter.21.cloned.1.call-update) | async-done | bytes 110608 | tf_op jit(solution)/shard_map/reduce_scatter | solution.py:132
  464.4 66.0 %reduce-scatter.19.cloned.1.call-done = bf16[96,576]{1,0:T(8,128)(2,1)} async-done(((bf16[768,576]{1,0:T(8,128)(2,1)}), bf16[96,576]{1,0:T(8,128)(2,1)}) %reduce-scatter.19.cloned.1.call-update) | async-done | bytes 110608 | tf_op jit(solution)/shard_map/reduce_scatter | solution.py:132
  530.4 1.8 convert_multiply_fusion.12
  532.1 65.2 %reduce-scatter.25.cloned.1.call-done = bf16[96,768]{1,0:T(8,128)(2,1)} async-done(((bf16[768,768]{1,0:T(8,128)(2,1)}), bf16[96,768]{1,0:T(8,128)(2,1)}) %reduce-scatter.25.cloned.1.call-update) | async-done | bytes 147472 | tf_op jit(solution)/shard_map/reduce_scatter | solution.py:132
  597.3 66.4 %reduce-scatter.23.cloned.1.call-done = bf16[96,768]{1,0:T(8,128)(2,1)} async-done(((bf16[768,768]{1,0:T(8,128)(2,1)}), bf16[96,768]{1,0:T(8,128)(2,1)}) %reduce-scatter.23.cloned.1.call-update) | async-done | bytes 147472 | tf_op jit(solution)/shard_map/reduce_scatter | solution.py:132
  663.7 1.8 convert_multiply_fusion.9
  665.6 64.6 %reduce-scatter.29.cloned.1.call-done = bf16[768,96]{0,1:T(8,128)(2,1)} async-done(((bf16[768,768]{0,1:T(8,128)(2,1)}), bf16[768,96]{0,1:T(8,128)(2,1)}) %reduce-scatter.29.cloned.1.call-update) | async-done | bytes 147472 | tf_op jit(solution)/shard_map/reduce_scatter | solution.py:132
  730.2 66.3 %reduce-scatter.27.cloned.1.call-done = bf16[768,96]{0,1:T(8,128)(2,1)} async-done(((bf16[768,768]{0,1:T(8,128)(2,1)}), bf16[768,96]{0,1:T(8,128)(2,1)}) %reduce-scatter.27.cloned.1.call-update) | async-done | bytes 147472 | tf_op jit(solution)/shard_map/reduce_scatter | solution.py:132
  796.5 1.8 convert_multiply_fusion.8
  (370 shorter events, 47.4 us)
Async XLA Ops:
  7.2 4.6 copy-start.120
  7.2 4.7 copy-start.100
  7.2 5.6 copy-start.42
  7.2 6.5 copy-start.56
  7.2 296.7 %reduce-scatter.33.cloned.1.call-start = ((), (), s32[]{:S(2)}) async-start(), calls=%async_computation.17 | async-start | bytes 73728
  8.8 60.9 %copy-start.83 = (f32[3,64]{1,0:T(4,128)}, f32[3,64]{1,0:T(4,128)S(1)}, u32[]{:S(2)}) copy-start(f32[3,64]{1,0:T(4,128)S(1)} %get-tuple-element.129) | copy-start | bytes 2308
  10.2 9.2 %copy-start.60 = (f32[592]{0:T(1024)}, f32[592]{0:T(1024)S(1)}, u32[]{:S(2)}) copy-start(f32[592]{0:T(1024)S(1)} %broadcast_multiply_fusion.11) | copy-start | bytes 7108
  11.8 7.6 copy-start.77
  11.9 8.8 %copy-start.81 = (f32[3,64]{1,0:T(4,128)}, f32[3,64]{1,0:T(4,128)S(1)}, u32[]{:S(2)}) copy-start(f32[3,64]{1,0:T(4,128)S(1)} %get-tuple-element.131) | copy-start | bytes 2308
  11.9 11.0 %copy-start.121 = (f32[3,64]{1,0:T(4,128)}, f32[3,64]{1,0:T(4,128)S(1)}, u32[]{:S(2)}) copy-start(f32[3,64]{1,0:T(4,128)S(1)} %get-tuple-element.132) | copy-start | bytes 2308
  12.8 10.1 %copy-start.24 = (pred[592,592]{0,1:T(8,128)(4,1)}, pred[592,592]{0,1:T(8,128)(4,1)S(1)}, u32[]{:S(2)}) copy-start(pred[592,592]{0,1:T(8,128)(4,1)S(1)} %fusion.61) | copy-start | bytes 1051396
  15.7 3.7 copy-start.33
  19.4 47.8 %copy-start.115 = (f32[768]{0:T(1024)}, f32[768]{0:T(1024)S(1)}, u32[]{:S(2)}) copy-start(f32[768]{0:T(1024)S(1)} %get-tuple-element.84) | copy-start | bytes 9220
  19.4 150.5 %copy-start.66 = (f32[768]{0:T(1024)}, f32[768]{0:T(1024)S(1)}, u32[]{:S(2)}) copy-start(f32[768]{0:T(1024)S(1)} %get-tuple-element.150) | copy-start | bytes 9220
  26.2 105.3 %copy-start.64 = (f32[768]{0:T(1024)}, f32[768]{0:T(1024)S(1)}, u32[]{:S(2)}) copy-start(f32[768]{0:T(1024)S(1)} %get-tuple-element.76) | copy-start | bytes 9220
  26.2 165.8 %copy-start.62 = (f32[768]{0:T(1024)}, f32[768]{0:T(1024)S(1)}, u32[]{:S(2)}) copy-start(f32[768]{0:T(1024)S(1)} %get-tuple-element.77) | copy-start | bytes 9220
  28.2 18.2 %copy-start.14 = (bf16[584,768]{1,0:T(8,128)(2,1)S(1)}, bf16[584,768]{1,0:T(8,128)(2,1)}, u32[]{:S(2)}) copy-start(bf16[584,768]{1,0:T(8,128)(2,1)} %param.15) | copy-start | bytes 2691076
  44.7 2.9 copy-start.46
  47.0 145.1 %copy-start.68 = (f32[592]{0:T(1024)}, f32[592]{0:T(1024)S(1)}, u32[]{:S(2)}) copy-start(f32[592]{0:T(1024)S(1)} %add_rsqrt_fusion.2) | copy-start | bytes 7108
  50.3 16.5 %copy-start.7 = (bf16[592,768]{1,0:T(8,128)(2,1)}, bf16[592,768]{1,0:T(8,128)(2,1)S(1)}, u32[]{:S(2)}) copy-start(bf16[592,768]{1,0:T(8,128)(2,1)S(1)} %get-tuple-element.135.x_ref) | copy-start | bytes 2727940
  66.8 4.0 copy-start.18
  67.2 102.7 %copy-start.72 = (f32[592]{0:T(1024)}, f32[592]{0:T(1024)S(1)}, u32[]{:S(2)}) copy-start(f32[592]{0:T(1024)S(1)} %add_rsqrt_fusion.1) | copy-start | bytes 7108
  74.4 20.1 %copy-start.53 = (bf16[3,64,592]{2,1,0:T(8,128)(2,1)}, bf16[3,64,592]{2,1,0:T(8,128)(2,1)S(1)}, u32[]{:S(2)}) copy-start(bf16[3,64,592]{2,1,0:T(8,128)(2,1)S(1)} %convolution_convert_fusion.11) | copy-start | bytes 681988
  94.5 37.0 %copy-start.21 = (f32[592,768]{1,0:T(8,128)}, f32[592,768]{1,0:T(8,128)S(1)}, u32[]{:S(2)}) copy-start(f32[592,768]{1,0:T(8,128)S(1)} %get-tuple-element.107) | copy-start | bytes 5455876
  94.9 36.7 %copy-start.70 = (f32[592]{0:T(1024)}, f32[592]{0:T(1024)S(1)}, u32[]{:S(2)}) copy-start(f32[592]{0:T(1024)S(1)} %add_rsqrt_fusion) | copy-start | bytes 7108
  96.6 19.6 %copy-start.9 = (bf16[592,768]{1,0:T(8,128)(2,1)}, bf16[592,768]{1,0:T(8,128)(2,1)S(1)}, u32[]{:S(2)}) copy-start(bf16[592,768]{1,0:T(8,128)(2,1)S(1)} %get-tuple-element.140.x_ref) | copy-start | bytes 2727940
  99.5 16.7 %copy-start.11 = (bf16[592,768]{1,0:T(8,128)(2,1)}, bf16[592,768]{1,0:T(8,128)(2,1)S(1)}, u32[]{:S(2)}) copy-start(bf16[592,768]{1,0:T(8,128)(2,1)S(1)} %get-tuple-element.117.x_ref) | copy-start | bytes 2727940
  116.2 15.4 %copy-start.95 = (f32[768]{0:T(1024)S(1)}, f32[768]{0:T(1024)}, u32[]{:S(2)}) copy-start(f32[768]{0:T(1024)} %get-tuple-element.72) | copy-start | bytes 9220
  116.2 20.5 %slice-start.2 = ((s8[4546560]{0:T(1024)(128)(4,1)}), s8[4194304]{0:T(1024)(128)(4,1)S(1)}, s32[]{:S(2)}) async-start(s8[4546560]{0:T(1024)(128)(4,1)} %bitcast.339), calls=%async_computation.22 | async-start | bytes 8388608
  131.6 3.0 copy-start.43
  131.6 5.2 slice-start.3
  142.1 3.8 copy-start.84
  144.1 160.6 %reduce-scatter.31.cloned.1.call-start = ((), (), s32[]{:S(2)}) async-start(), calls=%async_computation.16 | async-start | bytes 73728
  153.1 15.3 %copy-start.19 = (f32[592,768]{1,0:T(8,128)S(1)}, f32[592,768]{1,0:T(8,128)}, u32[]{:S(2)}) copy-start(f32[592,768]{1,0:T(8,128)} %copy-done.18) | copy-start | bytes 5455876
  169.9 3.0 copy-start.50
  169.9 3.0 copy-start.118
  169.9 3.0 copy-start.126
  172.9 19.2 %copy-start.29 = (f32[592,768]{1,0:T(8,128)}, f32[592,768]{1,0:T(8,128)S(1)}, u32[]{:S(2)}) copy-start(f32[592,768]{1,0:T(8,128)S(1)} %get-tuple-element.101) | copy-start | bytes 5455876
  175.2 15.3 %copy-start.15 = (bf16[584,768]{1,0:T(8,128)(2,1)S(1)}, bf16[584,768]{1,0:T(8,128)(2,1)}, u32[]{:S(2)}) copy-start(bf16[584,768]{1,0:T(8,128)(2,1)} %param.15) | copy-start | bytes 2691076
  190.5 5.0 slice-start
  192.1 3.4 slice-start.1
  202.5 132.1 %reduce-scatter.37.cloned.1.call-start = ((), (), s32[]{:S(2)}) async-start(), calls=%async_computation.19 | async-start | bytes 442368
  205.5 3.1 copy-start.36
  205.5 3.1 copy-start.67
  205.5 3.1 copy-start.73
  205.5 3.1 copy-start.116
  205.5 193.2 %reduce-scatter.35.cloned.1.call-start = ((), (), s32[]{:S(2)}) async-start(), calls=%async_computation.18 | async-start | bytes 442368
  208.5 4.0 copy-start.82
  208.5 255.9 %reduce-scatter.21.cloned.1.call-start = ((), (), s32[]{:S(2)}) async-start(), calls=%async_computation.11 | async-start | bytes 1105920 | tf_op jit(solution)/shard_map/reduce_scatter | solution.py:132
  212.4 318.0 %reduce-scatter.19.cloned.1.call-start = ((), (), s32[]{:S(2)}) async-start(), calls=%async_computation.10 | async-start | bytes 1105920 | tf_op jit(solution)/shard_map/reduce_scatter | solution.py:132
  218.7 4.1 copy-start.63
  218.7 4.1 copy-start.69
  218.7 4.1 copy-start.110
  218.7 378.6 %reduce-scatter.25.cloned.1.call-start = ((), (), s32[]{:S(2)}) async-start(), calls=%async_computation.13 | async-start | bytes 1327104 | tf_op jit(solution)/shard_map/reduce_scatter | solution.py:132
  222.7 3.9 copy-start.10
  222.7 441.0 %reduce-scatter.23.cloned.1.call-start = ((), (), s32[]{:S(2)}) async-start(), calls=%async_computation.12 | async-start | bytes 1327104 | tf_op jit(solution)/shard_map/reduce_scatter | solution.py:132
  226.6 3.8 copy-start.8
  226.6 503.6 %reduce-scatter.29.cloned.1.call-start = ((), (), s32[]{:S(2)}) async-start(), calls=%async_computation.15 | async-start | bytes 1327104 | tf_op jit(solution)/shard_map/reduce_scatter | solution.py:132
  230.1 4.0 copy-start.32
  230.1 566.4 %reduce-scatter.27.cloned.1.call-start = ((), (), s32[]{:S(2)}) async-start(), calls=%async_computation.14 | async-start | bytes 1327104 | tf_op jit(solution)/shard_map/reduce_scatter | solution.py:132
  235.9 16.9 %copy-start.17 = (bf16[584,768]{1,0:T(8,128)(2,1)S(1)}, bf16[584,768]{1,0:T(8,128)(2,1)}, u32[]{:S(2)}) copy-start(bf16[584,768]{1,0:T(8,128)(2,1)} %param.15) | copy-start | bytes 2691076
  235.9 16.9 %copy-start.76 = (f32[768]{0:T(1024)S(1)}, f32[768]{0:T(1024)}, u32[]{:S(2)}) copy-start(f32[768]{0:T(1024)} %copy-done.74) | copy-start | bytes 9220
  237.5 15.3 %copy-start.79 = (f32[592]{0:T(1024)S(1)}, f32[592]{0:T(1024)}, u32[]{:S(2)}) copy-start(f32[592]{0:T(1024)} %copy-done.77) | copy-start | bytes 7108
  252.9 45.3 %copy-start.80 = (f32[592]{0:T(1024)S(1)}, f32[592]{0:T(1024)}, u32[]{:S(2)}) copy-start(f32[592]{0:T(1024)} %copy-done.77) | copy-start | bytes 7108
  (77 other events, 146.4 us)
Sparse Core Ops, SparseCore 0:
  144.3 62.1 reduce-scatter.32
  209.9 60.2 reduce-scatter.30
  274.1 60.4 reduce-scatter.36
  338.3 60.3 reduce-scatter.34
  401.9 62.4 reduce-scatter.20
  468.0 62.3 reduce-scatter.18
  533.8 63.5 reduce-scatter.24
  600.7 62.9 reduce-scatter.22
  667.1 62.9 reduce-scatter.28
  733.4 62.9 reduce-scatter.26
